TPU v7x, 256 devices: a whole 4x4x8 slice. The times are simulated.
256 devices in a mesh: row: 32 (over y, z), col: 8 (over x, core).
Axes of the slice: x: 4, y: 4, z: 8, core: 2. Of those that a mesh axis runs over, the one named last changes fastest.
Arguments:
- queries: bfloat16 [16384, 1024], P(('row', 'col'))
- passages: bfloat16 [32768, 1024], P(('col', 'row'))
- positives: int32 [16384], P('row'), may hold values from 0 to 32767
Outputs:
- losses: float32 [16384], P('row')
- query_grad: float32 [16384, 1024], P(('row', 'col'))
- passage_grad: float32 [32768, 1024], P(('col', 'row'))
All inputs are finite; a program needn't handle non-finite values.
Results may differ from a plain program's by a relative error of at most 0.0022.
Values may be sent and summed in bfloat16 or wider, within the bound.
No kernel may reach another device: no remote copies, remote signals or barrier semaphores. Data moves between devices by JAX's collectives and lax.ppermute only.
A program may use at most 128 MiB of HBM per device.

v0:
```python
import math
import jax
import jax.numpy as jnp
from jax import lax
from jax.sharding import PartitionSpec as P

D = 1024


def body(queries, passages, positives):
    scale = 3.0 / math.sqrt(D)
    query_full = lax.all_gather(queries, "col", axis=0, tiled=True)
    passage_full = lax.all_gather(passages, "row", axis=0, tiled=True)
    scores = (
        lax.dot_general(
            query_full, passage_full, (((1,), (1,)), ((), ())), preferred_element_type=jnp.float32
        )
        * scale
    )
    passage_count = passage_full.shape[0]
    first_column = lax.axis_index("col") * passage_count
    column = lax.broadcasted_iota(jnp.int32, scores.shape, 1) + first_column
    hit = column == positives[:, None]
    local_score = jnp.sum(jnp.where(hit, scores, 0.0), axis=1)
    top = lax.pmax(jnp.max(scores, axis=1), "col")
    total, pos_score = lax.psum(
        (jnp.sum(jnp.exp(scores - top[:, None]), axis=1), local_score), "col"
    )
    lse = top + jnp.log(total)
    losses = lse - pos_score
    weights = ((jnp.exp(scores - lse[:, None]) - hit.astype(jnp.float32)) * scale).astype(
        jnp.bfloat16
    )
    query_grad = lax.psum_scatter(
        jnp.dot(weights, passage_full, preferred_element_type=jnp.float32),
        "col",
        scatter_dimension=0,
        tiled=True,
    )
    passage_grad = lax.psum_scatter(
        lax.dot_general(
            weights, query_full, (((0,), (0,)), ((), ())), preferred_element_type=jnp.float32
        ),
        "row",
        scatter_dimension=0,
        tiled=True,
    )
    return (losses, query_grad, passage_grad)


def solution(mesh):
    return jax.shard_map(
        body,
        mesh=mesh,
        in_specs=(P(("row", "col"), None), P(("col", "row"), None), P("row")),
        out_specs=(P("row"), P(("row", "col"), None), P(("col", "row"), None)),
        check_vma=False,
    )
```

profile of v0, /device:TPU:2, one launch (start us, length us, event | category | flops | bytes accessed | tf_op | source)
XLA Modules:
  0.0 483.9 jit_solution(17748731228473105264)
XLA Ops:
  7.2 0.0 all-gather.3.cloned.1.call-start
  7.2 0.7 all-gather.3.cloned.1.call-update
  7.9 0.0 all-gather.5.cloned.1.call-start
  7.9 0.7 all-gather.5.cloned.1.call-update
  8.6 0.0 reduce-scatter.3.cloned.1.call-start
  8.7 0.0 copy-start.1
  8.7 28.4 %all-gather.3.cloned.1.call-done = bf16[512,1024]{1,0:T(8,128)(2,1)} async-done(((bf16[64,1024]{1,0:T(8,128)(2,1)}), bf16[512,1024]{1,0:T(8,128)(2,1)}) %all-gather.3.cloned.1.call-update) | async-done | bytes 1048592 | tf_op jit(solution)/shard_map/all_gather | solution.py:12
  37.1 102.7 %all-gather.5.cloned.1.call-done = bf16[4096,1024]{1,0:T(8,128)(2,1)} async-done(((bf16[128,1024]{1,0:T(8,128)(2,1)}), bf16[4096,1024]{1,0:T(8,128)(2,1)}) %all-gather.5.cloned.1.call-update) | async-done | bytes 8388624 | tf_op jit(solution)/shard_map/all_gather | solution.py:13
  139.8 11.5 %multiply_reduce_fusion = (f32[512]{0:T(512)S(1)}, f32[512,4096]{1,0:T(8,128)}) fusion(bf16[512,1024]{1,0:T(8,128)(2,1)} %all-gather.3.cloned.1.call-done, bf16[4096,1024]{1,0:T(8,128)(2,1)} %all-gather.5.cloned.1.call-done), kind=kOutput, calls=%fused_computation.7 | convolution fusion | flops 4299161088 | bytes 17827840 | tf_op jit(solution)/shard_map/dot_general | solution.py:15
  151.3 11.2 %pmax.7 = f32[512]{0:T(512)S(1)} all-reduce(f32[512]{0:T(512)S(1)} %get-tuple-element.9), channel_id=1, replica_groups=mesh['row'=32,'col'=8] {'col'}, use_global_device_ids=true, to_apply=%region_1.2 | all-reduce | flops 512 | bytes 4096 | tf_op jit(solution)/shard_map/pmax | solution.py:25
  162.4 0.0 copy-done.1
  162.5 5.0 %fusion = (f32[512]{0:T(512)S(1)}, f32[512]{0:T(512)S(1)}) fusion(f32[512,4096]{1,0:T(8,128)} %get-tuple-element.10, s32[4096]{0:T(1024)S(1)} %iota_add_fusion, s32[512]{0:T(512)S(1)} %copy-done.1, f32[512]{0:T(512)S(1)} %pmax.7), kind=kLoop, calls=%fused_computation.2 | loop fusion | flops 12581888 | bytes 8413184 | tf_op jit(solution)/shard_map/reduce_sum | solution.py:24
  167.5 12.4 %all-reduce = (f32[512]{0:T(512)S(1)}, f32[512]{0:T(512)S(1)}) all-reduce(f32[512]{0:T(512)S(1)} %get-tuple-element.4, f32[512]{0:T(512)S(1)} %get-tuple-element.3), channel_id=1, replica_groups=mesh['row'=32,'col'=8] {'col'}, use_global_device_ids=true, to_apply=%region_3.4 | all-reduce | flops 1024 | bytes 8192 | tf_op jit(solution)/shard_map/psum | solution.py:26
  179.9 0.6 fusion.4
  180.5 4.8 fusion.3
  185.4 0.0 copy-start
  185.4 1.9 copy-done
  187.3 0.0 copy-start.2
  187.3 8.3 %fusion.5 = f32[512,1024]{1,0:T(8,128)} fusion(bf16[512,4096]{1,0:T(8,128)(2,1)S(1)} %fusion.3, bf16[4096,1024]{1,0:T(8,128)(2,1)} %all-gather.5.cloned.1.call-done), kind=kOutput, calls=%fused_computation.11 | convolution fusion | flops 4294967296 | bytes 14680064 | tf_op jit(solution)/shard_map/dot_general | solution.py:35
  195.6 0.0 reduce-scatter.3.cloned.1.call-update
  195.6 0.0 reduce-scatter.5.cloned.1.call-start
  195.6 0.0 copy-done.2
  195.7 10.6 %fusion.6 = f32[4096,1024]{1,0:T(8,128)} fusion(bf16[512,4096]{1,0:T(8,128)(2,1)} %copy-done, bf16[512,1024]{1,0:T(8,128)(2,1)S(1)} %copy-done.2), kind=kOutput, calls=%fused_computation.12 | convolution fusion | flops 4294967296 | bytes 22020096 | tf_op jit(solution)/shard_map/dot_general | solution.py:41
  206.2 0.0 reduce-scatter.5.cloned.1.call-update
  206.3 20.0 %reduce-scatter.3.cloned.1.call-done = f32[64,1024]{1,0:T(8,128)} async-done(((f32[512,1024]{1,0:T(8,128)}), f32[64,1024]{1,0:T(8,128)}) %reduce-scatter.3.cloned.1.call-update) | async-done | bytes 262160 | tf_op jit(solution)/shard_map/reduce_scatter | solution.py:34
  226.2 251.1 %reduce-scatter.5.cloned.1.call-done = f32[128,1024]{1,0:T(8,128)} async-done(((f32[4096,1024]{1,0:T(8,128)}), f32[128,1024]{1,0:T(8,128)}) %reduce-scatter.5.cloned.1.call-update) | async-done | bytes 524304 | tf_op jit(solution)/shard_map/reduce_scatter | solution.py:40
  (1 shorter events, 0.0 us)
Async XLA Ops:
  7.2 29.9 %all-gather.3.cloned.1.call-start = ((), (), s32[]{:S(2)}) async-start(), calls=%async_computation.2 | async-start | bytes 1179648 | tf_op jit(solution)/shard_map/all_gather | solution.py:12
  7.9 131.9 %all-gather.5.cloned.1.call-start = ((), (), s32[]{:S(2)}) async-start(), calls=%async_computation.3 | async-start | bytes 8650752 | tf_op jit(solution)/shard_map/all_gather | solution.py:13
  8.6 217.6 %reduce-scatter.3.cloned.1.call-start = ((), (), s32[]{:S(2)}) async-start(), calls=%async_computation.4 | async-start | bytes 2359296 | tf_op jit(solution)/shard_map/reduce_scatter | solution.py:34
  8.7 153.7 %copy-start.1 = (s32[512]{0:T(512)S(1)}, s32[512]{0:T(512)}, u32[]{:S(2)}) copy-start(s32[512]{0:T(512)} %param.5) | copy-start | bytes 6148
  185.4 1.9 copy-start
  187.3 8.4 %copy-start.2 = (bf16[512,1024]{1,0:T(8,128)(2,1)S(1)}, bf16[512,1024]{1,0:T(8,128)(2,1)}, u32[]{:S(2)}) copy-start(bf16[512,1024]{1,0:T(8,128)(2,1)} %all-gather.3.cloned.1.call-done) | copy-start | bytes 3145732
  195.6 281.7 %reduce-scatter.5.cloned.1.call-start = ((), (), s32[]{:S(2)}) async-start(), calls=%async_computation.5 | async-start | bytes 17301504 | tf_op jit(solution)/shard_map/reduce_scatter | solution.py:40
Sparse Core Ops, SparseCore 0:
  9.9 27.1 all-gather.2
  39.7 100.0 all-gather.4
  195.7 30.4 reduce-scatter.2
  230.8 246.5 reduce-scatter.4
where the time goes:
time: 484 us
  waiting for transfers between devices  404 us (83%)
  matrix products  30.3 us (6%)
  blocking collectives  23.6 us (5%)
  between operations  13.8 us (3%)
  other arithmetic  10.5 us (2%)
    reduce_scatter x1, waiting for transfers between devices, body(): lax.psum_scatter(lax.dot_general(weights, query_full, (((0,), (0,)), ((),...  251 us
    all_gather x1, waiting for transfers between devices, body(): passage_full = lax.all_gather(passages, 'row', axis=0, tiled=True)  103 us
    all_gather x1, waiting for transfers between devices, body(): query_full = lax.all_gather(queries, 'col', axis=0, tiled=True)  28.4 us
    reduce_scatter x1, waiting for transfers between devices, body(): lax.psum_scatter(jnp.dot(weights, passage_full, preferred_element_type=jn...  20 us
    psum x1, blocking collectives, body(): lax.psum((jnp.sum(jnp.exp(scores - top[:, None]), axis=1), local_score),...  12.4 us
    dot_general x1, matrix products, body(): lax.dot_general(query_full, passage_full, (((1,), (1,)), ((), ())), prefe...  11.5 us
    pmax x1, blocking collectives, body(): top = lax.pmax(jnp.max(scores, axis=1), 'col')  11.2 us
    dot_general x1, matrix products, body(): lax.dot_general(weights, query_full, (((0,), (0,)), ((), ())), preferred_...  10.6 us
  transfers between devices with their start and end apart: 4, of which 4 were waited for; matrix products, arithmetic and copies ran while one was open for 2% of the time, Pallas kernels for 0%

commit v1 on v0

--- a/solution.py
+++ b/solution.py
@@ -7,9 +7,14 @@
 D = 1024
 
 
+def gather_over(array, name, along):
+    sent = jnp.stack([array] * lax.axis_size(name))
+    return jnp.concatenate(lax.all_to_all(sent, name, 0, 0), axis=along)
+
+
 def body(queries, passages, positives):
     scale = 3.0 / math.sqrt(D)
-    query_full = lax.all_gather(queries, "col", axis=0, tiled=True)
+    query_full = gather_over(queries, "col", 0)
     passage_full = lax.all_gather(passages, "row", axis=0, tiled=True)
     scores = (
         lax.dot_general(

time: 484 us -> 455 us (0.940)
  waiting for transfers between devices: 404 us -> 369 us
  starting transfers between devices: 0.16 us -> 5.82 us
    all_gather x1 -> x0, waiting for transfers between devices: 28.4 us -> none  [body(): query_full = lax.all_gather(queries, 'col', axis=0, tiled=True)]
    all_gather x1, waiting for transfers between devices: 103 us -> 81.8 us  [body(): passage_full = lax.all_gather(passages, 'row', axis=0, tiled=True)]
    all_to_all x0 -> x1, waiting for transfers between devices: none -> 14.5 us  [gather_over(): return jnp.concatenate(lax.all_to_all(sent, name, 0, 0), axis=along)]
    all_to_all x0 -> x1, starting transfers between devices: none -> 5.74 us  [gather_over(): return jnp.concatenate(lax.all_to_all(sent, name, 0, 0), axis=along)]
  transfers between devices with their start and end apart: 4 -> 4, of which waited for: 4 -> 4; matrix products, arithmetic and copies ran while one was open for 2% -> 3% of each run, Pallas kernels for 0% -> 0%
where the time goes in v1:
time: 455 us
  waiting for transfers between devices  369 us (81%)
  matrix products  29 us (6%)
  blocking collectives  23.6 us (5%)
  between operations  13.8 us (3%)
  other arithmetic  10.5 us (2%)
  starting transfers between devices  5.82 us (1%)
    reduce_scatter x1, waiting for transfers between devices, body(): lax.psum_scatter(lax.dot_general(weights, query_full, (((0,), (0,)), ((),...  251 us
    all_gather x1, waiting for transfers between devices, body(): passage_full = lax.all_gather(passages, 'row', axis=0, tiled=True)  81.8 us
    reduce_scatter x1, waiting for transfers between devices, body(): lax.psum_scatter(jnp.dot(weights, passage_full, preferred_element_type=jn...  20 us
    all_to_all x1, waiting for transfers between devices, gather_over(): return jnp.concatenate(lax.all_to_all(sent, name, 0, 0), axis=along)  14.5 us
    psum x1, blocking collectives, body(): lax.psum((jnp.sum(jnp.exp(scores - top[:, None]), axis=1), local_score),...  12.4 us
    pmax x1, blocking collectives, body(): top = lax.pmax(jnp.max(scores, axis=1), 'col')  11.2 us
    dot_general x1, matrix products, body(): lax.dot_general(weights, query_full, (((0,), (0,)), ((), ())), preferred_...  10.6 us
    dot_general x1, matrix products, body(): lax.dot_general(query_full, passage_full, (((1,), (1,)), ((), ())), prefe...  10.2 us
  transfers between devices with their start and end apart: 4, of which 4 were waited for; matrix products, arithmetic and copies ran while one was open for 3% of the time, Pallas kernels for 0%

profile of v1, /device:TPU:2, one launch (start us, length us, event | category | flops | bytes accessed | tf_op | source)
XLA Modules:
  0.0 455.2 jit_solution(17937576922104830614)
XLA Ops:
  7.2 0.0 all-gather.2.cloned.1.call-start
  7.2 0.7 all-gather.2.cloned.1.call-update
  7.9 2.1 stack.2
  10.0 5.7 %all-to-all-start = ((bf16[8,64,1024]{2,1,0:T(8,128)(2,1)}), bf16[8,64,1024]{2,1,0:T(8,128)(2,1)S(1)}, u32[]{:S(2)}, u32[]{:S(2)}) async-start(bf16[8,64,1024]{2,1,0:T(8,128)(2,1)} %stack.2), calls=%async_computation | async-start | bytes 2097152 | tf_op jit(solution)/shard_map/all_to_all | solution.py:12
  15.7 0.0 reduce-scatter.3.cloned.1.call-start
  15.7 14.5 %all-to-all-done = bf16[8,64,1024]{2,1,0:T(8,128)(2,1)S(1)} async-done(((bf16[8,64,1024]{2,1,0:T(8,128)(2,1)}), bf16[8,64,1024]{2,1,0:T(8,128)(2,1)S(1)}, u32[]{:S(2)}, u32[]{:S(2)}) %all-to-all-start) | async-done | bytes 1048608 | tf_op jit(solution)/shard_map/all_to_all | solution.py:12
  30.3 81.8 %all-gather.2.cloned.1.call-done = bf16[4096,1024]{1,0:T(8,128)(2,1)} async-done(((bf16[128,1024]{1,0:T(8,128)(2,1)}), bf16[4096,1024]{1,0:T(8,128)(2,1)}) %all-gather.2.cloned.1.call-update) | async-done | bytes 8388624 | tf_op jit(solution)/shard_map/all_gather | solution.py:18
  112.1 0.0 copy-start.1
  112.1 10.2 %multiply_reduce_fusion = (f32[512]{0:T(512)S(1)}, f32[512,4096]{1,0:T(8,128)}) fusion(bf16[512,1024]{1,0:T(8,128)(2,1)S(1)} %bitcast.7, bf16[4096,1024]{1,0:T(8,128)(2,1)} %all-gather.2.cloned.1.call-done), kind=kOutput, calls=%fused_computation.7 | convolution fusion | flops 4299161088 | bytes 17827840 | tf_op jit(solution)/shard_map/dot_general | solution.py:20
  122.3 11.2 %pmax.7 = f32[512]{0:T(512)S(1)} all-reduce(f32[512]{0:T(512)S(1)} %get-tuple-element.9), channel_id=1, replica_groups=mesh['row'=32,'col'=8] {'col'}, use_global_device_ids=true, to_apply=%region_1.2 | all-reduce | flops 512 | bytes 4096 | tf_op jit(solution)/shard_map/pmax | solution.py:30
  133.5 0.0 copy-done.1
  133.5 5.0 %fusion = (f32[512]{0:T(512)S(1)}, f32[512]{0:T(512)S(1)}) fusion(f32[512,4096]{1,0:T(8,128)} %get-tuple-element.10, s32[4096]{0:T(1024)S(1)} %iota_add_fusion, s32[512]{0:T(512)S(1)} %copy-done.1, f32[512]{0:T(512)S(1)} %pmax.7), kind=kLoop, calls=%fused_computation.2 | loop fusion | flops 12581888 | bytes 8413184 | tf_op jit(solution)/shard_map/reduce_sum | solution.py:29
  138.5 12.4 %all-reduce = (f32[512]{0:T(512)S(1)}, f32[512]{0:T(512)S(1)}) all-reduce(f32[512]{0:T(512)S(1)} %get-tuple-element.4, f32[512]{0:T(512)S(1)} %get-tuple-element.3), channel_id=1, replica_groups=mesh['row'=32,'col'=8] {'col'}, use_global_device_ids=true, to_apply=%region_3.4 | all-reduce | flops 1024 | bytes 8192 | tf_op jit(solution)/shard_map/psum | solution.py:31
  150.9 0.6 fusion.4
  151.5 4.8 %fusion.3 = bf16[512,4096]{1,0:T(8,128)(2,1)S(1)} fusion(f32[512,4096]{1,0:T(8,128)} %get-tuple-element.10, f32[512]{0:T(512)S(1)} %get-tuple-element.8, s32[4096]{0:T(1024)S(1)} %iota_add_fusion, s32[512]{0:T(512)S(1)} %copy-done.1), kind=kLoop, calls=%fused_computation.5 | loop fusion | flops 14680064 | bytes 12603392 | tf_op jit(solution)/shard_map/convert_element_type | solution.py:36
  156.4 0.0 copy-start
  156.4 1.9 copy-done
  158.3 8.2 %fusion.5 = f32[512,1024]{1,0:T(8,128)} fusion(bf16[512,4096]{1,0:T(8,128)(2,1)S(1)} %fusion.3, bf16[4096,1024]{1,0:T(8,128)(2,1)} %all-gather.2.cloned.1.call-done), kind=kOutput, calls=%fused_computation.11 | convolution fusion | flops 4294967296 | bytes 14680064 | tf_op jit(solution)/shard_map/dot_general | solution.py:40
  166.5 0.0 reduce-scatter.3.cloned.1.call-update
  166.5 0.0 reduce-scatter.5.cloned.1.call-start
  166.6 10.6 %fusion.6 = f32[4096,1024]{1,0:T(8,128)} fusion(bf16[512,4096]{1,0:T(8,128)(2,1)} %copy-done, bf16[512,1024]{1,0:T(8,128)(2,1)S(1)} %bitcast.8), kind=kOutput, calls=%fused_computation.12 | convolution fusion | flops 4294967296 | bytes 22020096 | tf_op jit(solution)/shard_map/dot_general | solution.py:46
  177.2 0.0 reduce-scatter.5.cloned.1.call-update
  177.2 20.0 %reduce-scatter.3.cloned.1.call-done = f32[64,1024]{1,0:T(8,128)} async-done(((f32[512,1024]{1,0:T(8,128)}), f32[64,1024]{1,0:T(8,128)}) %reduce-scatter.3.cloned.1.call-update) | async-done | bytes 262160 | tf_op jit(solution)/shard_map/reduce_scatter | solution.py:39
  197.2 251.5 %reduce-scatter.5.cloned.1.call-done = f32[128,1024]{1,0:T(8,128)} async-done(((f32[4096,1024]{1,0:T(8,128)}), f32[128,1024]{1,0:T(8,128)}) %reduce-scatter.5.cloned.1.call-update) | async-done | bytes 524304 | tf_op jit(solution)/shard_map/reduce_scatter | solution.py:45
  (1 shorter events, 0.0 us)
Async XLA Ops:
  7.2 104.9 %all-gather.2.cloned.1.call-start = ((), (), s32[]{:S(2)}) async-start(), calls=%async_computation.3 | async-start | bytes 8650752 | tf_op jit(solution)/shard_map/all_gather | solution.py:18
  10.0 20.3 %all-to-all-start = ((bf16[8,64,1024]{2,1,0:T(8,128)(2,1)}), bf16[8,64,1024]{2,1,0:T(8,128)(2,1)S(1)}, u32[]{:S(2)}, u32[]{:S(2)}) async-start(bf16[8,64,1024]{2,1,0:T(8,128)(2,1)} %stack.2), calls=%async_computation | async-start | bytes 2097152 | tf_op jit(solution)/shard_map/all_to_all | solution.py:12
  15.7 181.5 %reduce-scatter.3.cloned.1.call-start = ((), (), s32[]{:S(2)}) async-start(), calls=%async_computation.4 | async-start | bytes 2359296 | tf_op jit(solution)/shard_map/reduce_scatter | solution.py:39
  112.1 21.4 %copy-start.1 = (s32[512]{0:T(512)S(1)}, s32[512]{0:T(512)}, u32[]{:S(2)}) copy-start(s32[512]{0:T(512)} %param.5) | copy-start | bytes 6148
  156.4 1.9 copy-start
  166.5 282.1 %reduce-scatter.5.cloned.1.call-start = ((), (), s32[]{:S(2)}) async-start(), calls=%async_computation.5 | async-start | bytes 17301504 | tf_op jit(solution)/shard_map/reduce_scatter | solution.py:45
Sparse Core Ops, SparseCore 0:
  10.6 101.4 all-gather.1
  166.6 30.4 reduce-scatter.2
  201.9 246.7 reduce-scatter.4
